TPU v7x, 32 devices: a whole 2x2x4 slice. The times are simulated.
32 devices in a mesh: seq: 8 (over y, x, core), head: 4 (over z).
Axes of the slice: x: 2, y: 2, z: 4, core: 2. Of those that a mesh axis runs over, the one named last changes fastest.
Arguments:
- tokens: bfloat16 [4096, 1152], P(('seq', 'head')), may hold values from -6 to 6
- segment_ids: int32 [4096], replicated, may hold values from 0 to 5, as said below
- w_query: bfloat16 [1152, 1024], replicated, may hold values from -0.1875 to 0.1875
- w_key: bfloat16 [1152, 256], replicated, may hold values from -0.1875 to 0.1875
- w_value: bfloat16 [1152, 256], replicated, may hold values from -0.1875 to 0.1875
- w_out: bfloat16 [1024, 1152], replicated, may hold values from -0.1875 to 0.1875
- w_gate: bfloat16 [1152, 6912], P(None, 'head'), may hold values from -0.1875 to 0.1875
- w_up: bfloat16 [1152, 6912], P(None, 'head'), may hold values from -0.1875 to 0.1875
- w_down: bfloat16 [6912, 1152], P('head'), may hold values from -0.078125 to 0.078125
- gain_attn_in: float32 [1152], replicated, may hold values from 0.25 to 1.75
- gain_attn_out: float32 [1152], replicated, may hold values from 0.25 to 1.75
- gain_ffn_in: float32 [1152], replicated, may hold values from 0.25 to 1.75
- gain_ffn_out: float32 [1152], replicated, may hold values from 0.25 to 1.75
- gain_query: float32 [256], replicated, may hold values from 0.25 to 1.75
- gain_key: float32 [256], replicated, may hold values from 0.25 to 1.75
- cotangent: bfloat16 [4096, 1152], P(('seq', 'head'))
Outputs:
- output: bfloat16 [4096, 1152], P(('seq', 'head'))
- grad_tokens: bfloat16 [4096, 1152], P(('seq', 'head'))
- grad_w_query: float32 [1152, 1024], P(('seq', 'head'))
- grad_w_key: float32 [1152, 256], P(('seq', 'head'))
- grad_w_value: float32 [1152, 256], P(('seq', 'head'))
- grad_w_out: float32 [1024, 1152], P(('seq', 'head'))
- grad_w_gate: float32 [1152, 6912], P('seq', 'head')
- grad_w_up: float32 [1152, 6912], P('seq', 'head')
- grad_w_down: float32 [6912, 1152], P('head', 'seq')
- grad_gain_attn_in: float32 [1152], P(('seq', 'head'))
- grad_gain_attn_out: float32 [1152], P(('seq', 'head'))
- grad_gain_ffn_in: float32 [1152], P(('seq', 'head'))
- grad_gain_ffn_out: float32 [1152], P(('seq', 'head'))
- grad_gain_query: float32 [256], P(('seq', 'head'))
- grad_gain_key: float32 [256], P(('seq', 'head'))
Inputs may be any that keep to these rules, and one draw needn't show every extreme that they name: `segment_ids`: nonzero ids never decrease and each forms one run; id 0 marks padding, one run at the end of the row; id 2 runs from within the first 512 tokens into the last 512.
All inputs are finite; a program needn't handle non-finite values.
Results may differ from a plain program's by a relative error of at most 0.024.
Values may be sent and summed in bfloat16 or wider, within the bound.
A program may use at most 192 MiB of HBM per device.

v0:
```python
import functools
import itertools
import math

import jax
import jax.numpy as jnp
from jax import lax
from jax.experimental import pallas as pl
from jax.experimental.pallas import tpu as pltpu
from jax.sharding import PartitionSpec as P

EPS = 1e-06
MESH = pl.DeviceIdType.MESH
VMEM = pltpu.VMEM
LIMIT = 56 * 2**20


def norm_rows(v, gain):
    return v * lax.rsqrt(jnp.mean(v * v, axis=-1, keepdims=True) + EPS) * gain


def rotate(v, cosines, sines):
    half = v.shape[-1] // 2
    first = v[..., :half]
    second = v[..., half:]
    return jnp.concatenate(
        [first * cosines - second * sines, second * cosines + first * sines], axis=-1
    )


def rope_tables(positions, width):
    half = width // 2
    freq = jnp.exp(jnp.arange(half, dtype=jnp.float32) * (-2.0 * math.log(1000000.0) / width))
    angle = positions.astype(jnp.float32)[:, None] * freq[None, :]
    return (jnp.cos(angle), jnp.sin(angle))


def contract_first(left, right):
    return lax.dot_general(
        left, right, (((0,), (0,)), ((), ())), preferred_element_type=jnp.float32
    )


def contract_last(left, right):
    return lax.dot_general(
        left, right, (((1,), (1,)), ((), ())), preferred_element_type=jnp.float32
    )


def place():
    return lax.axis_index("seq"), lax.axis_index("head")


def related(s, mask):
    out = s
    bit = 0
    while mask >> bit:
        if (mask >> bit) & 1:
            step = 1 << bit
            out = out + (1 - 2 * ((s // step) % 2)) * step
        bit += 1
    return out


def subsets(bits):
    out = [0]
    for bit in bits:
        out = out + [m | (1 << bit) for m in out]
    return out


def greet(targets):
    barrier = pltpu.get_barrier_semaphore()
    for target in targets:
        pl.semaphore_signal(barrier, inc=1, device_id=target, device_id_type=MESH)
    pl.semaphore_wait(barrier, len(targets))


def remote(src, dst, send, recv, target):
    return pltpu.make_async_remote_copy(
        src_ref=src,
        dst_ref=dst,
        send_sem=send,
        recv_sem=recv,
        device_id=target,
        device_id_type=MESH,
    )


def seq_orders(bits):
    upper = list(range(1, bits))
    return upper, upper[::-1]


def gather_kernel(nseq, heads, local_refs, out_refs, send, recv):
    bits = nseq.bit_length() - 1
    s, h = place()
    others = [lax.rem(h + d, heads) for d in range(1, heads)]
    greet([(related(s, 1 << b), h) for b in range(bits)] + [(s, o) for o in others])
    count = [0]
    started = []

    def go(src, dst, target):
        k = count[0]
        count[0] += 1
        copy = remote(src, dst, send.at[k], recv.at[k], target)
        copy.start()
        started.append(copy)
        return copy

    first = []
    for a in range(len(out_refs)):
        out_refs[a][s, h] = local_refs[a][...]
        first.append(
            [go(local_refs[a], out_refs[a].at[s, h], (s, o)) for o in others]
        )
    orders = [o + [0] for o in seq_orders(bits)]
    held = [{0: first[a]} for a in range(len(out_refs))]
    for stage in range(bits):
        for a in range(len(out_refs)):
            bit = orders[a % 2][stage]
            target = (related(s, 1 << bit), h)
            arrived = {}
            for mask in list(held[a]):
                for copy in held[a][mask]:
                    copy.wait_recv()
                held[a][mask] = []
                group = related(s, mask)
                copy = go(out_refs[a].at[group], out_refs[a].at[group], target)
                arrived[mask | (1 << bit)] = [copy]
            held[a].update(arrived)
    for a in range(len(out_refs)):
        for mask in held[a]:
            for copy in held[a][mask]:
                copy.wait_recv()
    for copy in started:
        copy.wait_send()


def gather_all(arrays, nseq, heads, cid):
    n = len(arrays)
    total = n * (heads - 1 + nseq - 1)

    def kernel(*refs):
        gather_kernel(nseq, heads, refs[:n], refs[n : 2 * n], refs[2 * n], refs[2 * n + 1])

    return pl.pallas_call(
        kernel,
        out_shape=[jax.ShapeDtypeStruct((nseq, heads) + a.shape, a.dtype) for a in arrays],
        in_specs=[pl.BlockSpec(memory_space=VMEM)] * n,
        out_specs=[pl.BlockSpec(memory_space=VMEM)] * n,
        scratch_shapes=[pltpu.SemaphoreType.DMA((total,)), pltpu.SemaphoreType.DMA((total,))],
        name="gather_all",
        compiler_params=pltpu.CompilerParams(
            collective_id=cid, has_side_effects=True, vmem_limit_bytes=LIMIT
        ),
    )(*arrays)


def line_gather_kernel(heads, x_ref, out_ref, send, recv):
    s, h = place()
    right = (s, lax.rem(h + 1, heads))
    left = (s, lax.rem(h + heads - 1, heads))
    greet([right, left])
    out_ref[h] = x_ref[...]
    for step in range(heads - 1):
        to_right = remote(
            out_ref.at[jnp.maximum(h - step, 0)],
            out_ref.at[jnp.maximum(h - step, 0)],
            send.at[0, step],
            recv.at[0, step],
            right,
        )
        to_left = remote(
            out_ref.at[jnp.minimum(h + step, heads - 1)],
            out_ref.at[jnp.minimum(h + step, heads - 1)],
            send.at[1, step],
            recv.at[1, step],
            left,
        )
        pl.when((h - step >= 0) & (h < heads - 1))(to_right.start)
        pl.when((h + step <= heads - 1) & (h > 0))(to_left.start)
        pl.when(h - 1 - step >= 0)(
            remote(
                out_ref.at[jnp.maximum(h - 1 - step, 0)],
                out_ref.at[jnp.maximum(h - 1 - step, 0)],
                send.at[0, step],
                recv.at[0, step],
                right,
            ).wait_recv
        )
        pl.when(h + 1 + step <= heads - 1)(
            remote(
                out_ref.at[jnp.minimum(h + 1 + step, heads - 1)],
                out_ref.at[jnp.minimum(h + 1 + step, heads - 1)],
                send.at[1, step],
                recv.at[1, step],
                left,
            ).wait_recv
        )
        pl.when((h - step >= 0) & (h < heads - 1))(to_right.wait_send)
        pl.when((h + step <= heads - 1) & (h > 0))(to_left.wait_send)


def line_gather(x, heads, cid):
    return pl.pallas_call(
        functools.partial(line_gather_kernel, heads),
        out_shape=jax.ShapeDtypeStruct((heads,) + x.shape, x.dtype),
        in_specs=[pl.BlockSpec(memory_space=VMEM)],
        out_specs=pl.BlockSpec(memory_space=VMEM),
        scratch_shapes=[
            pltpu.SemaphoreType.DMA((2, heads - 1)),
            pltpu.SemaphoreType.DMA((2, heads - 1)),
        ],
        name="line_gather",
        compiler_params=pltpu.CompilerParams(
            collective_id=cid, has_side_effects=True, vmem_limit_bytes=LIMIT
        ),
    )(x)


def line_scatter_kernel(heads, parts, out_ref, from_left, from_right, send, recv):
    s, h = place()
    last = heads - 1
    right = (s, lax.rem(h + 1, heads))
    left = (s, lax.rem(h + heads - 1, heads))
    greet([right, left])
    f32 = jnp.float32
    for step in range(heads - 1):
        r_dest = jnp.clip(last - (step - h), 0, last)
        l_dest = jnp.clip(step - (last - h), 0, last)
        r_on = (step >= h) & (h < last)
        l_on = (step >= last - h) & (h > 0)
        for on, dest, box, lane, target, first in (
            (r_on, r_dest, from_left, 0, right, step == h),
            (l_on, l_dest, from_right, 1, left, step == last - h),
        ):
            at_end = (h == 0) if lane == 0 else (h == last)
            if step > 0:

                def add(box=box, dest=dest):
                    box[step - 1] = (
                        box[step - 1].astype(f32) + parts[dest].astype(f32)
                    ).astype(box.dtype)

                pl.when(on & jnp.logical_not(at_end))(add)
                pl.when(on & jnp.logical_not(at_end))(
                    remote(
                        box.at[step - 1], box.at[step], send.at[lane, step], recv.at[lane, step], target
                    ).start
                )
            pl.when(on & at_end)(
                remote(
                    parts.at[dest], box.at[step], send.at[lane, step], recv.at[lane, step], target
                ).start
            )
        r_in = (step >= h - 1) & (h > 0)
        l_in = (step >= last - h - 1) & (h < last)
        pl.when(r_in)(
            remote(
                from_left.at[step], from_left.at[step], send.at[0, step], recv.at[0, step], right
            ).wait_recv
        )
        pl.when(l_in)(
            remote(
                from_right.at[step], from_right.at[step], send.at[1, step], recv.at[1, step], left
            ).wait_recv
        )
    for step in range(heads - 1):
        for on, box, lane, target in (
            ((step >= h) & (h < last), from_left, 0, right),
            ((step >= last - h) & (h > 0), from_right, 1, left),
        ):
            pl.when(on)(
                remote(
                    box.at[step], box.at[step], send.at[lane, step], recv.at[lane, step], target
                ).wait_send
            )
    out_ref[...] = parts[h].astype(f32)

    def add_left():
        out_ref[...] += from_left[heads - 2].astype(f32)

    def add_right():
        out_ref[...] += from_right[heads - 2].astype(f32)

    pl.when(h > 0)(add_left)
    pl.when(h < last)(add_right)


def line_scatter(parts, heads, cid):
    block = parts.shape[1:]
    return pl.pallas_call(
        functools.partial(line_scatter_kernel, heads),
        out_shape=jax.ShapeDtypeStruct(block, jnp.float32),
        in_specs=[pl.BlockSpec(memory_space=VMEM)],
        out_specs=pl.BlockSpec(memory_space=VMEM),
        scratch_shapes=[
            VMEM((heads - 1,) + block, parts.dtype),
            VMEM((heads - 1,) + block, parts.dtype),
            pltpu.SemaphoreType.DMA((2, heads - 1)),
            pltpu.SemaphoreType.DMA((2, heads - 1)),
        ],
        name="line_scatter",
        compiler_params=pltpu.CompilerParams(
            collective_id=cid, has_side_effects=True, vmem_limit_bytes=LIMIT
        ),
    )(parts)


def scatter_kernel(nseq, heads, zs, orders, parts, outs, boxes, zboxes, send, recv):
    bits = nseq.bit_length() - 1
    s, h = place()
    f32 = jnp.float32
    others = [lax.rem(h + d, heads) for d in range(1, heads)]
    greet(
        [(related(s, 1 << b), h) for b in range(bits)]
        + ([(s, o) for o in others] if any(zs) else [])
    )
    count = [0]
    started = []

    def go(src, dst, target):
        k = count[0]
        count[0] += 1
        copy = remote(src, dst, send.at[k], recv.at[k], target)
        copy.start()
        started.append(copy)
        return copy

    n = len(parts)
    offsets = [0] * n
    slot = [{} for _ in range(n)]
    waiting = [{} for _ in range(n)]

    def current(a, mask):
        if mask in slot[a]:
            return boxes[a].at[slot[a][mask]]
        return parts[a].at[related(s, mask)]

    def launch(a, stage):
        bit = orders[a][stage]
        rest = orders[a][stage + 1 :]
        target = (related(s, 1 << bit), h)
        after = 1 << rest[0] if rest else 0
        masks = sorted(subsets(rest), key=lambda m: 0 if m & after else 1)
        for mask in masks:
            where = offsets[a]
            offsets[a] += 1
            waiting[a][mask] = (
                go(current(a, mask | (1 << bit)), boxes[a].at[where], target),
                where,
            )

    def settle(a, mask):
        copy, where = waiting[a].pop(mask)
        mine = current(a, mask)
        copy.wait_recv()
        boxes[a][where] = (boxes[a][where].astype(f32) + mine[...].astype(f32)).astype(
            boxes[a].dtype
        )
        slot[a][mask] = where

    for a in range(n):
        launch(a, 0)
    for stage in range(bits):
        for a in range(n):
            for mask in list(waiting[a]):
                settle(a, mask)
            if stage + 1 < bits:
                launch(a, stage + 1)
    arriving = []
    for a in range(n):
        if not zs[a]:
            continue
        mine = current(a, 0)
        arriving.append(
            [
                go(mine.at[o], zboxes[a].at[d], (s, o))
                for d, o in enumerate(others)
            ]
        )
    z = 0
    for a in range(n):
        if zs[a]:
            total = current(a, 0)[h].astype(f32)
            for d, copy in enumerate(arriving[z]):
                copy.wait_recv()
                total = total + zboxes[a][d].astype(f32)
            outs[a][...] = total
            z += 1
        else:
            outs[a][...] = current(a, 0)[...].astype(f32)
    for copy in started:
        copy.wait_send()


def scatter_all(arrays, zs, orders, nseq, heads, cid, name):
    n = len(arrays)
    total = sum((nseq - 1) + (heads - 1 if z else 0) for z in zs)
    blocks = [a.shape[2:] if z else a.shape[1:] for a, z in zip(arrays, zs)]

    def kernel(*refs):
        scatter_kernel(
            nseq,
            heads,
            zs,
            orders,
            refs[:n],
            refs[n : 2 * n],
            refs[2 * n : 3 * n],
            refs[3 * n : 4 * n],
            refs[4 * n],
            refs[4 * n + 1],
        )

    return pl.pallas_call(
        kernel,
        out_shape=[jax.ShapeDtypeStruct(b, jnp.float32) for b in blocks],
        in_specs=[pl.BlockSpec(memory_space=VMEM)] * n,
        out_specs=[pl.BlockSpec(memory_space=VMEM)] * n,
        scratch_shapes=[VMEM((nseq - 1,) + a.shape[1:], a.dtype) for a in arrays]
        + [
            VMEM((heads - 1,) + b, a.dtype) if z else VMEM((8, 128), jnp.float32)
            for a, b, z in zip(arrays, blocks, zs)
        ]
        + [pltpu.SemaphoreType.DMA((total,)), pltpu.SemaphoreType.DMA((total,))],
        name=name,
        compiler_params=pltpu.CompilerParams(
            collective_id=cid, has_side_effects=True, vmem_limit_bytes=LIMIT
        ),
    )(*arrays)


def attend_kernel(q_ref, k_ref, v_ref, start_ref, index_ref, out_ref, log_ref):
    s = lax.axis_index("seq")
    span = k_ref.shape[1]
    start = start_ref[...]
    index = index_ref[...]
    queries = q_ref[...]
    rows = queries.shape[0]
    out_ref[...] = jnp.zeros_like(out_ref)

    def step(g, mass):
        scores = contract_last(k_ref[g], queries)
        key = g * span + lax.broadcasted_iota(jnp.int32, (span, rows), 0)
        terms = jnp.where((key >= start) & (key <= index), jnp.exp(scores), 0.0)
        out_ref[...] += contract_first(v_ref[g], terms.astype(jnp.bfloat16))
        return mass + jnp.sum(terms, axis=0, keepdims=True)

    mass = lax.fori_loop(0, s + 1, step, jnp.zeros((1, rows), jnp.float32))
    out_ref[...] = out_ref[...] / mass
    log_ref[...] = jnp.log(mass)


def attend(q, k, v, start, index):
    rows, width = q.shape
    return pl.pallas_call(
        attend_kernel,
        out_shape=[
            jax.ShapeDtypeStruct((width, rows), jnp.float32),
            jax.ShapeDtypeStruct((1, rows), jnp.float32),
        ],
        in_specs=[pl.BlockSpec(memory_space=VMEM)] * 5,
        out_specs=[pl.BlockSpec(memory_space=VMEM)] * 2,
        name="attend",
        compiler_params=pltpu.CompilerParams(vmem_limit_bytes=LIMIT),
    )(q, k, v, start, index)


def attend_back_kernel(
    q_ref, k_ref, v_ref, start_ref, index_ref, log_ref, dots_ref, d_ref, dq_ref, dk_ref, dv_ref
):
    s = lax.axis_index("seq")
    groups, span = k_ref.shape[:2]
    start = start_ref[...]
    index = index_ref[...]
    log_total = log_ref[...]
    dots = dots_ref[...]
    queries = q_ref[...]
    grads = d_ref[...]
    rows = queries.shape[0]
    dq_ref[...] = jnp.zeros_like(dq_ref)

    def step(g, carry):
        keys = k_ref[g]
        scores = contract_last(keys, queries)
        key = g * span + lax.broadcasted_iota(jnp.int32, (span, rows), 0)
        probs = jnp.where((key >= start) & (key <= index), jnp.exp(scores - log_total), 0.0)
        d_probs = contract_last(v_ref[g], grads)
        d_scores = (probs * (d_probs - dots)).astype(jnp.bfloat16)
        dv_ref[g] = jnp.dot(
            probs.astype(jnp.bfloat16), grads, preferred_element_type=jnp.float32
        ).astype(dv_ref.dtype)
        dk_ref[g] = jnp.dot(d_scores, queries, preferred_element_type=jnp.float32).astype(
            dk_ref.dtype
        )
        dq_ref[...] += contract_first(keys, d_scores)
        return carry

    lax.fori_loop(0, s + 1, step, 0)

    def blank(g, carry):
        dk_ref[g] = jnp.zeros(dk_ref.shape[1:], dk_ref.dtype)
        dv_ref[g] = jnp.zeros(dv_ref.shape[1:], dv_ref.dtype)
        return carry

    lax.fori_loop(s + 1, groups, blank, 0)


def attend_back(q, k, v, start, index, log_total, dots, grads):
    rows, width = q.shape
    return pl.pallas_call(
        attend_back_kernel,
        out_shape=[
            jax.ShapeDtypeStruct((width, rows), jnp.float32),
            jax.ShapeDtypeStruct(k.shape, jnp.bfloat16),
            jax.ShapeDtypeStruct(v.shape, jnp.bfloat16),
        ],
        in_specs=[pl.BlockSpec(memory_space=VMEM)] * 8,
        out_specs=[pl.BlockSpec(memory_space=VMEM)] * 3,
        name="attend_back",
        compiler_params=pltpu.CompilerParams(vmem_limit_bytes=LIMIT),
    )(q, k, v, start, index, log_total, dots, grads)


def flat(ref):
    return ref[...].reshape(1, ref.shape[0])


def front_kernel(
    nseq,
    heads,
    qcount,
    scale,
    x_ref,
    ids_ref,
    w_key_ref,
    w_value_ref,
    gain_in_ref,
    gain_q_ref,
    gain_k_ref,
    w_query_far,
    w_out_far,
    o_proj,
    o_q,
    o_k,
    o_v,
    o_start,
    o_index,
    o_log,
    o_att,
    o_q_lin,
    o_k_lin,
    o_cos,
    o_sin,
    o_attn_t,
    w_query,
    w_out,
    k_all,
    v_all,
    send,
    recv,
    local_sem,
):
    f32, bf16 = jnp.float32, jnp.bfloat16
    bits = nseq.bit_length() - 1
    ups, downs = seq_orders(bits)
    links = Links(nseq, heads, send, recv)
    s, h = links.s, links.h
    rows, model = x_ref.shape
    width = w_key_ref.shape[1]
    gain_q, gain_k = flat(gain_q_ref), flat(gain_k_ref)
    half = width // 2
    total = ids_ref.shape[0] * ids_ref.shape[1]
    load_q = pltpu.make_async_copy(w_query_far, w_query, local_sem.at[0])
    load_q.start()
    load_o = pltpu.make_async_copy(w_out_far, w_out, local_sem.at[1])
    load_o.start()
    partners = [related(h, j) for j in range(1, heads)]
    greet([links.across(b) for b in range(bits)] + [(s, o) for o in partners])

    which = s * heads + h
    mine = ids_ref[pl.ds(which, 1), :].astype(f32)
    column = jnp.broadcast_to(mine, (rows, rows)).T[:, 0:1]
    first = jnp.full((rows, rows), float(total), f32)
    for r in range(ids_ref.shape[0]):
        here = ids_ref[r : r + 1, :].astype(f32)
        at = (r * rows + lax.broadcasted_iota(jnp.int32, (1, rows), 1)).astype(f32)
        first = jnp.minimum(first, jnp.where(column == here, at, float(total)))
    start = jnp.min(first, axis=1, keepdims=True)
    index = (which * rows + lax.broadcasted_iota(jnp.int32, (rows, 1), 0)).astype(f32)
    freq = jnp.exp(
        lax.broadcasted_iota(jnp.int32, (1, half), 1).astype(f32)
        * (-2.0 * math.log(1000000.0) / width)
    )
    angle = (index - start) * freq
    turns = jnp.round(angle * (1.0 / (2.0 * math.pi)))
    angle = (angle - turns * 6.28125) - turns * (2.0 * math.pi - 6.28125)
    cosines, sines = jnp.cos(angle), jnp.sin(angle)
    o_cos[...] = cosines
    o_sin[...] = sines
    start_row = jnp.broadcast_to(start, (rows, rows)).T[0:1, :].astype(jnp.int32)
    index_row = which * rows + lax.broadcasted_iota(jnp.int32, (1, rows), 1)
    for j in range(qcount):
        o_start[:, pl.ds(j * rows, rows)] = start_row
        o_index[:, pl.ds(j * rows, rows)] = index_row

    attn_in = norm_rows(x_ref[...].astype(f32), flat(gain_in_ref)).astype(bf16)
    k_lin = jnp.dot(attn_in, w_key_ref[...], preferred_element_type=f32)
    k_all[s, h] = rotate(norm_rows(k_lin, gain_k), cosines, sines).astype(bf16)
    o_k_lin[...] = k_lin
    v_all[s, h] = jnp.dot(attn_in, w_value_ref[...], preferred_element_type=f32).astype(bf16)

    both = ((k_all, ups), (v_all, downs))

    def pass_on(a, mask, j, bit):
        buf = both[a][0]
        block = buf.at[related(s, mask), related(h, j)]
        return links.go(block, block, links.across(bit))

    over_head = {}
    for j in range(1, heads):
        for a in range(2):
            block = both[a][0].at[s, h]
            over_head[a, j] = links.go(block, block, (s, partners[j - 1]))
    arriving = {}

    def spread(a, mask, j, stage):
        order = both[a][1]
        for later in range(stage, len(order)):
            bit = order[later]
            arriving[a, mask | (1 << bit), j] = pass_on(a, mask, j, bit)

    for a in range(2):
        spread(a, 0, 0, 0)

    load_q.wait()
    q_lin = jnp.dot(attn_in, w_query[...], preferred_element_type=f32)
    o_q_lin[...] = q_lin
    for j in range(1, heads):
        for a in range(2):
            over_head[a, j].wait_recv()
            spread(a, 0, j, 0)
    for j in range(qcount):
        part = norm_rows(q_lin[:, j * width : (j + 1) * width], gain_q)
        o_q[pl.ds(j * rows, rows), :] = (rotate(part, cosines, sines) * scale).astype(bf16)

    pairs = []

    def to_pair(a, mask):
        block = both[a][0].at[related(s, mask)]
        pairs.append(links.go(block, block, links.across(0)))

    for a in range(2):
        to_pair(a, 0)
    for stage in range(len(ups)):
        for lower in subsets(range(stage)):
            masks = []
            for a in range(2):
                order = both[a][1]
                mask = sum(1 << order[i] for i in range(stage) if lower >> i & 1)
                masks.append(mask | (1 << order[stage]))
            for j in range(heads):
                for a in range(2):
                    arriving[a, masks[a], j].wait_recv()
                    spread(a, masks[a], j, stage + 1)
            for a in range(2):
                to_pair(a, masks[a])
    for j in range(1):
        o_attn_t[...] = attn_in.T.reshape(o_attn_t.shape)

    queries = o_q[...]
    starts = o_start[...]
    indices = o_index[...]
    o_att[...] = jnp.zeros_like(o_att)
    span = heads * rows
    low = lax.rem(s, 2)

    def attend_group(g, mass):
        scores = contract_last(k_all[g].reshape(span, width), queries)
        key = g * span + lax.broadcasted_iota(jnp.int32, scores.shape, 0)
        terms = jnp.where((key >= starts) & (key <= indices), jnp.exp(scores), 0.0)
        o_att[...] += contract_first(v_all[g].reshape(span, width), terms.astype(bf16))
        return mass + jnp.sum(terms, axis=0, keepdims=True)

    mass = lax.fori_loop(
        0,
        s // 2 + 1,
        lambda i, m: attend_group(2 * i + low, m),
        jnp.zeros((1, qcount * rows), f32),
    )
    for copy in pairs:
        copy.wait_recv()
    mass = lax.fori_loop(
        0, s // 2 + low, lambda i, m: attend_group(2 * i + 1 - low, m), mass
    )
    keep_k = pltpu.make_async_copy(k_all, o_k, local_sem.at[2])
    keep_v = pltpu.make_async_copy(v_all, o_v, local_sem.at[3])
    keep_k.start()
    keep_v.start()
    o_log[...] = jnp.log(mass)
    attended = o_att[...] / mass
    o_att[...] = attended
    load_o.wait()
    proj = jnp.zeros((rows, model), f32)
    for j in range(qcount):
        part = attended[:, j * rows : (j + 1) * rows].T.astype(bf16)
        proj = proj + jnp.dot(
            part, w_out[pl.ds(j * width, width), :], preferred_element_type=f32
        )
    o_proj[...] = proj
    keep_k.wait()
    keep_v.wait()
    links.finish()


def front(nseq, heads, qcount, scale, cid, x, ids, w_key, w_value, gain_in, gain_q, gain_k, w_query, w_out):
    f32, bf16, i32 = jnp.float32, jnp.bfloat16, jnp.int32
    rows, model = x.shape
    width = w_key.shape[1]
    stacked = qcount * rows
    some = nseq // 2
    messages = 2 * (heads - 1) + 2 * heads * (some - 1) + 2 * some
    vm = pl.BlockSpec(memory_space=VMEM)
    anywhere = pl.BlockSpec(memory_space=pl.ANY)
    everyone = (nseq, heads, rows, width)

    def kernel(*refs):
        front_kernel(nseq, heads, qcount, scale, *refs)

    shape = jax.ShapeDtypeStruct
    return pl.pallas_call(
        kernel,
        out_shape=[
            shape((rows, model), f32),
            shape((stacked, width), bf16),
            shape(everyone, bf16),
            shape(everyone, bf16),
            shape((1, stacked), i32),
            shape((1, stacked), i32),
            shape((1, stacked), f32),
            shape((width, stacked), f32),
            shape((rows, qcount * width), f32),
            shape((rows, width), f32),
            shape((rows, width // 2), f32),
            shape((rows, width // 2), f32),
            shape((nseq, model // nseq, rows), bf16),
        ],
        in_specs=[vm] * 7 + [anywhere] * 2,
        out_specs=[vm] * 2 + [anywhere] * 2 + [vm] * 9,
        scratch_shapes=[
            VMEM(w_query.shape, bf16),
            VMEM(w_out.shape, bf16),
            VMEM(everyone, bf16),
            VMEM(everyone, bf16),
            pltpu.SemaphoreType.DMA((messages,)),
            pltpu.SemaphoreType.DMA((messages,)),
            pltpu.SemaphoreType.DMA((4,)),
        ],
        name="front",
        compiler_params=pltpu.CompilerParams(
            collective_id=cid, has_side_effects=True, vmem_limit_bytes=LIMIT
        ),
    )(
        x,
        ids.reshape(nseq * heads, rows),
        w_key,
        w_value,
        gain_in,
        gain_q,
        gain_k,
        w_query,
        w_out,
    )


class Sum:
    def __init__(self, links, part, boxes, order):
        self.links, self.part, self.boxes, self.order = links, part, boxes, order
        self.used = 0
        self.slot = {}
        self.waiting = {}

    def current(self, mask):
        if mask in self.slot:
            return self.boxes.at[self.slot[mask]]
        return self.part(mask)

    def masks(self, stage):
        rest = self.order[stage + 1 :]
        weight = lambda m: sum(1 << (len(rest) - i) for i, b in enumerate(rest) if m >> b & 1)
        return sorted(subsets(rest), key=weight, reverse=True)

    def send(self, stage, mask):
        bit = self.order[stage]
        where = self.used
        self.used += 1
        copy = self.links.go(
            self.current(mask | (1 << bit)), self.boxes.at[where], self.links.across(bit)
        )
        self.waiting[stage, mask] = (copy, where)

    def start(self):
        for mask in self.masks(0):
            self.send(0, mask)

    def steps(self, stage, kept=None):
        def step(mask):
            copy, where = self.waiting.pop((stage, mask))
            mine = kept(mask) if kept is not None else self.current(mask)
            copy.wait_recv()
            self.boxes[where] = self.boxes[where] + mine[...]
            self.slot[mask] = where
            if stage + 1 < len(self.order):
                bit = 1 << self.order[stage + 1]
                if mask & bit:
                    self.send(stage + 1, mask & ~bit)

        return [functools.partial(step, mask) for mask in self.masks(stage)]

    def last(self, kept=None):
        copy, where = self.waiting.pop((len(self.order) - 1, 0))
        mine = kept(0) if kept is not None else self.current(0)
        copy.wait_recv()
        return self.boxes[where].astype(jnp.float32) + mine[...].astype(jnp.float32)


def in_turn(*lists):
    for group in itertools.zip_longest(*lists):
        for step in group:
            if step is not None:
                step()


def split_rows(rows):
    return (rows // 2 + 15) // 16 * 16


class Links:
    def __init__(self, nseq, heads, send, recv):
        self.s, self.h = place()
        self.nseq, self.heads = nseq, heads
        self.send, self.recv = send, recv
        self.count = 0
        self.started = []
        self.others = [lax.rem(self.h + d, heads) for d in range(1, heads)]

    def greet(self, more=()):
        bits = self.nseq.bit_length() - 1
        near = [self.across(b) for b in range(bits)]
        greet(near + [(self.s, o) for o in self.others] + list(more))

    def across(self, bit):
        return (related(self.s, 1 << bit), self.h)

    def go(self, src, dst, target):
        k = self.count
        self.count += 1
        copy = remote(src, dst, self.send.at[k], self.recv.at[k], target)
        copy.start()
        self.started.append(copy)
        return copy

    def over_heads(self, src, boxes):
        return [self.go(src.at[o], boxes.at[d], (self.s, o)) for d, o in enumerate(self.others)]

    def finish(self):
        for copy in self.started:
            copy.wait_send()


def back_norm(v, gain, d_out):
    scale = lax.rsqrt(jnp.mean(v * v, axis=-1, keepdims=True) + EPS)
    unit = v * scale
    inner = d_out * gain
    d_v = scale * (inner - unit * jnp.mean(inner * unit, axis=-1, keepdims=True))
    return d_v, jnp.sum(d_out * unit, axis=0, keepdims=True)


def back_rotate(d, cosines, sines):
    half = d.shape[-1] // 2
    first, second = d[:, :half], d[:, half:]
    return jnp.concatenate(
        [first * cosines + second * sines, second * cosines - first * sines], axis=-1
    )


def tail_kernel(
    nseq,
    heads,
    qcount,
    scale,
    q_ref,
    start_ref,
    index_ref,
    log_ref,
    att_ref,
    d_proj_ref,
    k_lin_ref,
    cos_ref,
    sin_ref,
    gain_q_ref,
    gain_k_ref,
    gain_in_ref,
    gains_ref,
    k_far,
    v_far,
    w_out_far,
    q_lin_far,
    attn_t_far,
    x_far,
    d_hid_far,
    w_query_far,
    w_key_far,
    w_value_far,
    d_gate_ref,
    d_up_ref,
    d_down_first,
    d_down_second,
    o_tokens,
    o_qkv,
    o_out,
    o_gate,
    o_up,
    o_down,
    o_gains,
    k_ref,
    v_ref,
    w_out_ref,
    q_lin_ref,
    attn_t_ref,
    x_ref,
    d_hid_ref,
    w_qkv_ref,
    dk,
    dv,
    dq_t,
    grads,
    grads_t,
    box_k,
    box_v,
    zbox_k,
    zbox_v,
    dw_out,
    box_out,
    zbox_out,
    mid_out,
    end_out,
    dw_qkv,
    box_qkv,
    zsrc_qkv,
    zbox_qkv,
    d_qkv,
    keep_gate_first,
    keep_gate_second,
    keep_up_first,
    keep_up_second,
    keep_down_first,
    keep_down_second,
    box_gate_first,
    box_gate_second,
    box_up_first,
    box_up_second,
    box_down_first,
    box_down_second,
    gsum,
    gbox,
    gzbox,
    send,
    recv,
    local_sem,
):
    f32, bf16 = jnp.float32, jnp.bfloat16
    bits = nseq.bit_length() - 1
    ups, downs = seq_orders(bits)
    links = Links(nseq, heads, send, recv)
    s, h = links.s, links.h
    rows, model = d_proj_ref.shape
    width = k_lin_ref.shape[1]
    gain_q, gain_k = flat(gain_q_ref), flat(gain_k_ref)
    groups, span = k_ref.shape[:2]
    loads = []

    def load(src, dst):
        copy = pltpu.make_async_copy(src, dst, local_sem.at[len(loads)])
        copy.start()
        loads.append(copy)
        return copy

    load_o = load(w_out_far, w_out_ref)
    load_k = load(k_far, k_ref)
    load_v = load(v_far, v_ref)
    plane = subsets(ups)[1:]
    links.greet([(related(s, m), links.h) for m in plane if m & (m - 1)])

    held = subsets(ups)
    ffn = []
    split = keep_gate_first.shape[1]
    for src, keep, box, order, low, past in (
        (d_gate_ref, keep_gate_first, box_gate_first, ups, 0, 1),
        (d_gate_ref, keep_gate_second, box_gate_second, downs, split, 1),
        (d_up_ref, keep_up_first, box_up_first, [0] + ups, 0, 0),
        (d_up_ref, keep_up_second, box_up_second, [0] + downs, split, 0),
        (d_down_first, keep_down_first, box_down_first, ups[1:], 0, 2),
        (d_down_second, keep_down_second, box_down_second, downs[1:], 0, 2),
    ):
        here = pl.ds(low, keep.shape[1])

        def part(m, src=src, here=here, past=past, order=order):
            if past == 0:
                return src.at[related(s, m), here]
            if past == 1:
                return src.at[held.index(m), here]
            return src.at[0 if m else 1, here]

        total = Sum(links, part, box, order)
        kept = subsets(order[1:])
        total.loads = [load(part(m), keep.at[i]) for i, m in enumerate(kept)]
        total.kept = lambda m, keep=keep, kept=kept: keep.at[kept.index(m)]
        ffn.append(total)
    gate, up, down = ffn[0:2], ffn[2:4], ffn[4:6]
    for total in up + gate + down:
        total.start()

    def settle(pair, stage, first=False):
        if first:
            for total in pair:
                for copy in total.loads:
                    copy.wait()
        in_turn(*[total.steps(stage, total.kept if first else None) for total in pair])

    def put(pair, out, first=False):
        at = 0
        for total in pair:
            value = total.last(total.kept if first else None).astype(out.dtype)
            out[pl.ds(at, value.shape[0]), :] = value
            at += value.shape[0]

    load_q = load(q_lin_far, q_lin_ref)
    load_a = load(attn_t_far, attn_t_ref)
    load_x = load(x_far, x_ref)
    load_d = load(d_hid_far, d_hid_ref)
    load_w = []
    at = 0
    for far in (w_query_far, w_key_far, w_value_far):
        load_w.append(load(far, w_qkv_ref.at[:, pl.ds(at, far.shape[1])]))
        at += far.shape[1]

    d_proj = d_proj_ref[...]

    out_rows = dw_out.shape[1] * dw_out.shape[2]

    def out_block(j, carry):
        low = pl.multiple_of((j * out_rows) % width, out_rows)
        head = pl.multiple_of((j * out_rows) // width * rows, rows)
        mixed_t = att_ref[pl.ds(low, out_rows), pl.ds(head, rows)].astype(bf16)
        dw_out[j] = (
            jnp.dot(mixed_t, d_proj, preferred_element_type=f32)
            .astype(bf16)
            .reshape(dw_out.shape[1:])
        )
        return carry

    lax.fori_loop(0, nseq, out_block, 0)
    sum_out = Sum(links, lambda m: dw_out.at[related(s, m)], box_out, [0])
    sum_out.masks = lambda stage: held
    sum_out.start()

    load_o.wait()

    def back_out(j, carry):
        part = w_out_ref[pl.ds(pl.multiple_of(j * width, width), width), :]
        here = pl.ds(pl.multiple_of(j * rows, rows), rows)
        grads[here, :] = contract_last(d_proj, part).astype(bf16)
        grads_t[:, here] = contract_last(part, d_proj).astype(bf16)
        return carry

    lax.fori_loop(0, qcount, back_out, 0)
    in_turn(sum_out.steps(0))
    z_out = [
        links.go(box_out.at[:, o], zbox_out.at[d], (s, o)) for d, o in enumerate(links.others)
    ]
    dots = jnp.sum(grads_t[...].astype(f32) * att_ref[...], axis=0, keepdims=True)
    start = start_ref[...]
    index = index_ref[...]
    log_total = log_ref[...]
    dq_t[...] = jnp.zeros_like(dq_t)
    load_k.wait()
    load_v.wait()

    def step(g, carry):
        keys = k_ref[g]
        queries = q_ref[...]
        scores = contract_last(keys, queries)
        key = g * span + lax.broadcasted_iota(jnp.int32, scores.shape, 0)
        probs = jnp.where((key >= start) & (key <= index), jnp.exp(scores - log_total), 0.0)
        d_probs = jnp.dot(v_ref[g], grads_t[...], preferred_element_type=f32)
        d_scores = (probs * (d_probs - dots)).astype(bf16)
        dv[g] = (
            jnp.dot(probs.astype(bf16), grads[...], preferred_element_type=f32)
            .astype(bf16)
            .reshape(dv.shape[1:])
        )
        dk[g] = (
            jnp.dot(d_scores, queries, preferred_element_type=f32)
            .astype(bf16)
            .reshape(dk.shape[1:])
        )
        dq_t[...] += contract_first(keys, d_scores)
        return carry

    def blank(g, carry):
        dk[g] = jnp.zeros(dk.shape[1:], bf16)
        dv[g] = jnp.zeros(dv.shape[1:], bf16)
        return carry

    lax.fori_loop(0, s + 1, step, 0)
    lax.fori_loop(s + 1, groups, blank, 0)

    kv = []
    for j in list(range(1, heads)) + [0]:
        owner = lax.rem(h + j, heads)
        for far, box, order in ((dk, box_k, ups), (dv, box_v, downs)):
            kv.append(
                Sum(
                    links,
                    lambda m, far=far, owner=owner: far.at[related(s, m), owner],
                    box.at[j],
                    [0] + order,
                )
            )
    for mask_index in range(len(held)):
        for total in kv:
            total.send(0, total.masks(0)[mask_index])

    in_turn(*[total.steps(0) for total in kv])

    load_q.wait()
    cosines, sines = cos_ref[...], sin_ref[...]
    d_gain_q = jnp.zeros((1, width), f32)
    for j in range(qcount):
        d_rot = dq_t[:, pl.ds(j * rows, rows)].T * scale
        d_lin, terms = back_norm(
            q_lin_ref[:, pl.ds(j * width, width)],
            gain_q,
            back_rotate(d_rot, cosines, sines),
        )
        d_qkv[:, pl.ds(j * width, width)] = d_lin.astype(bf16)
        d_gain_q = d_gain_q + terms

    for stage in range(1, bits - 1):
        in_turn(*[total.steps(stage) for total in kv])
    settle(gate, 0, True)

    arriving = {}
    for i, total in enumerate(kv):
        for m in total.steps(bits - 1):
            m()
        j = (i // 2 + 1) % heads
        if j:
            zbox = (zbox_k, zbox_v)[i % 2]
            arriving[i % 2, j] = links.go(
                total.current(0), zbox.at[j - 1], (s, links.others[j - 1])
            )
    for d, copy in enumerate(z_out):
        copy.wait_recv()
    own = box_out[:, h].astype(f32)
    for d in range(heads - 1):
        own = own + zbox_out[d].astype(f32)
    mid_out[...] = own.astype(bf16)
    sum_end = Sum(links, lambda m: mid_out.at[held.index(m)], end_out, downs)
    sum_end.start()


    settle(up, 0, True)

    def whole(i, zbox):
        total = kv[len(kv) - 2 + i].current(0)[...].astype(f32)
        for j in range(1, heads):
            arriving[i, j].wait_recv()
            total = total + zbox[j - 1].astype(f32)
        return total

    d_keys = whole(0, zbox_k)
    d_lin, d_gain_k = back_norm(
        k_lin_ref[...], gain_k, back_rotate(d_keys, cosines, sines)
    )
    qw = qcount * width
    d_qkv[:, pl.ds(qw, width)] = d_lin.astype(bf16)
    d_values = whole(1, zbox_v)
    d_qkv[:, pl.ds(qw + width, width)] = d_values.astype(bf16)

    pieces, _, block_rows, cut = dw_qkv.shape
    load_a.wait()
    qkv = []
    for j in range(pieces):
        cols = pl.ds(j * cut, cut)

        def qkv_block(g, carry, j=j, cols=cols):
            dw_qkv[j, g] = jnp.dot(
                attn_t_ref[g], d_qkv[:, cols], preferred_element_type=f32
            ).astype(bf16)
            return carry

        lax.fori_loop(0, nseq, qkv_block, 0)
        total = Sum(
            links,
            lambda m, j=j: dw_qkv.at[j, related(s, m)],
            box_qkv.at[j],
            [0] + (downs if j % 2 else ups),
        )
        total.start()
        qkv.append(total)

    for copy in load_w + [load_x, load_d]:
        copy.wait()
    d_attn_in = contract_last(d_qkv[...], w_qkv_ref[...])
    in_turn(*[total.steps(0) for total in qkv])
    d_x, d_gain_in = back_norm(x_ref[...].astype(f32), flat(gain_in_ref), d_attn_in)
    o_tokens[...] = (d_hid_ref[...] + d_x).astype(o_tokens.dtype)

    gsum[0] = gains_ref[...]
    gsum[0, 0:1, :] = d_gain_in
    gsum[0, 4:5, :width] = d_gain_q
    gsum[0, 5:6, :width] = d_gain_k
    gain_copy = links.go(gsum.at[0], gbox.at[0], links.across(0))
    for stage in range(1, bits - 1):
        in_turn(*[total.steps(stage) for total in qkv])
    gain_copy.wait_recv()
    gsum[1] = gsum[0] + gbox[0]
    gain_plane = [
        links.go(gsum.at[1], gbox.at[1 + i], (related(s, m), h)) for i, m in enumerate(plane)
    ]
    in_turn(sum_end.steps(0))
    settle(up, 1)
    each = block_rows // heads
    z_qkv = []

    for j, total in enumerate(qkv):
        value = total.last()
        for p in range(heads):
            zsrc_qkv[j, p] = value[p * each : (p + 1) * each].astype(bf16)
        z_qkv.append(links.over_heads(zsrc_qkv.at[j], zbox_qkv.at[j]))
    total_gains = gsum[1]
    for i, copy in enumerate(gain_plane):
        copy.wait_recv()
        total_gains = total_gains + gbox[1 + i]
    gsum[2] = total_gains
    gain_z = [
        links.go(gsum.at[2], gzbox.at[d], (s, o)) for d, o in enumerate(links.others)
    ]
    for total in down:
        for copy in total.loads:
            copy.wait()
    put(down, o_down, True)
    put(gate, o_gate)
    put(up, o_up)
    o_out[...] = sum_end.last()
    for j, copies in enumerate(z_qkv):
        total = zsrc_qkv[j, h].astype(f32)
        for d, copy in enumerate(copies):
            copy.wait_recv()
            total = total + zbox_qkv[j, d].astype(f32)
        o_qkv[:, pl.ds(j * cut, cut)] = total
    total = gsum[2]
    for d, copy in enumerate(gain_z):
        copy.wait_recv()
        total = total + gzbox[d]
    o_gains[...] = total
    links.finish()


def tail(nseq, heads, qcount, scale, cid, *arrays):
    (q, _, _, _, att, d_proj, k_lin, _, _, gain_q, _, _, gains, k, v) = arrays[:15]
    (w_out, q_lin, attn_t, x, d_hid, w_query, w_key, w_value, d_gate, _, _, _) = arrays[15:]
    f32, bf16 = jnp.float32, jnp.bfloat16
    rows, model = d_proj.shape
    width = k_lin.shape[1]
    cols = w_query.shape[1] + w_key.shape[1] + w_value.shape[1]
    pieces = 4
    cut = cols // pieces
    out_rows, qkv_rows = w_out.shape[0] // nseq, attn_t.shape[1]
    ffn_block = d_gate.shape[1:]
    some, all_but = nseq // 2, nseq - 1
    out_block = (heads, out_rows // heads, model)
    split = split_rows(ffn_block[0])
    low, high = (split, ffn_block[1]), (ffn_block[0] - split, ffn_block[1])
    parts = [(part, *n) for n in ((2, 3), (4, 7), (1, 1)) for part in (low, high)]
    copies = (
        sum(n for _, _, n in parts)
        + some
        + (heads - 1)
        + (some - 1)
        + 2 * heads * all_but
        + 2 * (heads - 1)
        + pieces * (all_but + heads - 1)
        + some
        + (heads - 1)
    )
    vm = pl.BlockSpec(memory_space=VMEM)
    anywhere = pl.BlockSpec(memory_space=pl.ANY)

    def kernel(*refs):
        tail_kernel(nseq, heads, qcount, scale, *refs)

    return pl.pallas_call(
        kernel,
        out_shape=[
            jax.ShapeDtypeStruct((rows, model), bf16),
            jax.ShapeDtypeStruct((qkv_rows // heads, cols), f32),
            jax.ShapeDtypeStruct(out_block[1:], f32),
            jax.ShapeDtypeStruct(ffn_block, bf16),
            jax.ShapeDtypeStruct(ffn_block, bf16),
            jax.ShapeDtypeStruct(ffn_block, bf16),
            jax.ShapeDtypeStruct(gains.shape, f32),
        ],
        in_specs=[vm] * 13 + [anywhere] * 14,
        out_specs=[vm] * 7,
        scratch_shapes=[
            VMEM(k.shape, bf16),
            VMEM(v.shape, bf16),
            *[VMEM(a.shape, a.dtype) for a in (w_out, q_lin, attn_t, x, d_hid)],
            VMEM((model, cols), bf16),
            VMEM((nseq, heads, rows, width), bf16),
            VMEM((nseq, heads, rows, width), bf16),
            VMEM((width, qcount * rows), f32),
            VMEM((qcount * rows, width), bf16),
            VMEM((width, qcount * rows), bf16),
            VMEM((heads, all_but, rows, width), bf16),
            VMEM((heads, all_but, rows, width), bf16),
            VMEM((heads - 1, rows, width), bf16),
            VMEM((heads - 1, rows, width), bf16),
            VMEM((nseq,) + out_block, bf16),
            VMEM((some,) + out_block, bf16),
            VMEM((heads - 1, some) + out_block[1:], bf16),
            VMEM((some,) + out_block[1:], bf16),
            VMEM((some - 1,) + out_block[1:], bf16),
            VMEM((pieces, nseq, qkv_rows, cut), bf16),
            VMEM((pieces, all_but, qkv_rows, cut), bf16),
            VMEM((pieces, heads, qkv_rows // heads, cut), bf16),
            VMEM((pieces, heads - 1, qkv_rows // heads, cut), bf16),
            VMEM((rows, cols), bf16),
        ]
        + [VMEM((n,) + part, bf16) for part, n, _ in parts]
        + [VMEM((n,) + part, bf16) for part, _, n in parts]
        + [
            VMEM((3,) + gains.shape, f32),
            VMEM((some,) + gains.shape, f32),
            VMEM((heads - 1,) + gains.shape, f32),
            pltpu.SemaphoreType.DMA((copies,)),
            pltpu.SemaphoreType.DMA((copies,)),
            pltpu.SemaphoreType.DMA((10 + sum(n for _, n, _ in parts),)),
        ],
        name="tail",
        compiler_params=pltpu.CompilerParams(
            collective_id=cid, has_side_effects=True, vmem_limit_bytes=62 * 2**20
        ),
    )(*arrays)


CHUNKS, SPANS = 4, 2
ORDER = (
    ("ags", 0, 0, 0), ("ags", 0, 1, 0), ("agw", 0, 0, 0), ("ags", 0, 0, 1), ("agw", 0, 1, 0),
    ("ags", 0, 1, 1), ("agw", 0, 0, 1), ("ags", 0, 0, 2), ("agw", 0, 1, 1), ("ags", 0, 1, 2),
    ("ags", 0, 3, 0), ("ags", 0, 2, 0), ("agw", 0, 1, 2), ("agw", 0, 0, 2), ("fa", 0), ("fb", 0),
    ("agw", 0, 3, 0), ("ags", 0, 3, 1), ("agw", 0, 2, 0), ("ags", 0, 2, 1), ("fc", 0),
    ("agw", 0, 3, 1), ("ags", 0, 3, 2), ("rss", 0, 0, 0), ("agw", 0, 2, 1), ("ags", 0, 2, 2),
    ("rsw", 0, 0, 0), ("rss", 0, 1, 0), ("rss", 0, 0, 1), ("rsw", 0, 1, 0), ("rss", 0, 1, 1),
    ("agw", 0, 3, 2), ("agw", 0, 2, 2), ("fa", 1), ("rsw", 0, 0, 1), ("rss", 0, 0, 2), ("fb", 1),
    ("rsw", 0, 1, 1), ("rss", 0, 1, 2), ("fc", 1), ("rss", 0, 2, 0), ("rsw", 0, 0, 2), ("n", 0),
    ("ags", 1, 0, 0), ("rss", 0, 3, 0), ("rsw", 0, 1, 2), ("rsw", 0, 2, 0), ("n", 1),
    ("rss", 0, 2, 1), ("ags", 1, 1, 0), ("agw", 1, 0, 0), ("rsw", 0, 3, 0), ("ags", 1, 0, 1),
    ("rss", 0, 3, 1), ("rsw", 0, 2, 1), ("rss", 0, 2, 2), ("agw", 1, 1, 0), ("ags", 1, 1, 1),
    ("agw", 1, 0, 1), ("ags", 1, 0, 2), ("rsw", 0, 3, 1), ("rss", 0, 3, 2), ("rsw", 0, 2, 2),
    ("n", 2), ("ags", 1, 2, 0), ("agw", 1, 1, 1), ("ags", 1, 1, 2), ("rsw", 0, 3, 2), ("n", 3),
    ("ags", 1, 3, 0), ("agw", 1, 0, 2), ("agw", 1, 2, 0), ("ags", 1, 2, 1), ("agw", 1, 1, 2),
    ("ga", 0), ("gb", 0), ("agw", 1, 3, 0), ("ags", 1, 3, 1), ("gc", 0), ("rss", 1, 1, 0),
    ("agw", 1, 2, 1), ("ags", 1, 2, 2), ("rss", 1, 0, 0), ("agw", 1, 3, 1), ("ags", 1, 3, 2),
    ("rsw", 1, 1, 0), ("rss", 1, 1, 1), ("agw", 1, 2, 2), ("agw", 1, 3, 2), ("wd", 0), ("wd", 1),
    ("dd", 0), ("rsw", 1, 0, 0), ("rsw", 1, 1, 1), ("rss", 1, 0, 1), ("rss", 1, 1, 2), ("ga", 1),
    ("gb", 1), ("gc", 1), ("rss", 1, 2, 0), ("Dd", 0), ("rsw", 1, 0, 1), ("rsw", 1, 1, 2),
    ("rss", 1, 3, 0), ("rss", 1, 0, 2), ("wg", 0), ("rsw", 1, 2, 0), ("e", 1), ("rss", 1, 2, 1),
    ("wg", 1), ("dg", 0), ("rsw", 1, 3, 0), ("rss", 1, 3, 1), ("rsw", 1, 0, 2), ("e", 0),
    ("rsw", 1, 2, 1), ("rss", 1, 2, 2), ("wu", 0), ("rsw", 1, 3, 1), ("rss", 1, 3, 2), ("wu", 1),
    ("rsw", 1, 2, 2), ("e", 2), ("Dg", 0), ("rsw", 1, 3, 2), ("e", 3), ("D2", 0),
)


def ffn_kernel(
    nseq,
    heads,
    chunks,
    spans,
    proj_ref,
    x_ref,
    cot_ref,
    gain_two_ref,
    gain_three_ref,
    gain_four_ref,
    w_gate_ref,
    w_up_ref,
    w_down_ref,
    o_out,
    o_hid,
    o_proj,
    o_gains,
    o_first,
    o_second,
    o_gate,
    o_up,
    hidden,
    w_gate,
    w_up,
    w_down,
    u_all,
    d_all,
    by_gate,
    by_up,
    act,
    d_gate,
    d_up,
    parts,
    from_left,
    from_right,
    flipped,
    dw_gate,
    dw_up,
    dw_down,
    box_gate,
    box_down,
    box_first,
    box_second,
    sum_send,
    sum_recv,
    ag_send,
    ag_recv,
    rs_send,
    rs_recv,
    local_sem,
):
    f32, bf16 = jnp.float32, jnp.bfloat16
    s, h = place()
    last = heads - 1
    right = (s, lax.rem(h + 1, heads))
    left = (s, lax.rem(h + last, heads))
    rows, model = x_ref.shape
    units = w_gate.shape[0]
    rc = rows // chunks
    each = chunks // spans
    many = rc * heads * each

    loads = []
    for n, (src, dst) in enumerate(
        ((w_gate_ref, w_gate), (w_up_ref, w_up), (w_down_ref, w_down))
    ):
        copy = pltpu.make_async_copy(src, dst, local_sem.at[n])
        copy.start()
        loads.append(copy)
    bits = nseq.bit_length() - 1
    ups, downs = seq_orders(bits)
    links = Links(nseq, heads, sum_send, sum_recv)
    greet([right, left] + [links.across(b) for b in range(bits)])

    proj = proj_ref[...]
    hid = x_ref[...].astype(f32) + norm_rows(proj, flat(gain_two_ref))
    hidden[...] = hid
    u_local = norm_rows(hid, flat(gain_three_ref)).astype(bf16)
    for c in range(chunks):
        u_all[c, h] = u_local[c * rc : (c + 1) * rc]
    o_gains[...] = jnp.zeros_like(o_gains)

    def lanes(k, c, t):
        buf = d_all if k else u_all
        return (
            (
                (h - t >= 0) & (h < last),
                buf.at[c, jnp.maximum(h - t, 0)],
                0,
                right,
                h - 1 - t >= 0,
                buf.at[c, jnp.maximum(h - 1 - t, 0)],
            ),
            (
                (h + t <= last) & (h > 0),
                buf.at[c, jnp.minimum(h + t, last)],
                1,
                left,
                h + 1 + t <= last,
                buf.at[c, jnp.minimum(h + 1 + t, last)],
            ),
        )

    def ags(k, c, t):
        for on, block, lane, target, _, _ in lanes(k, c, t):
            i = (k, c, lane, t)
            pl.when(on)(remote(block, block, ag_send.at[i], ag_recv.at[i], target).start)

    def agw(k, c, t):
        for _, _, lane, target, on, block in lanes(k, c, t):
            i = (k, c, lane, t)
            pl.when(on)(remote(block, block, ag_send.at[i], ag_recv.at[i], target).wait_recv)

    def rss(k, c, t):
        for on, dest, box, lane, target, at_end in (
            ((t >= h) & (h < last), last - (t - h), from_left, 0, right, h == 0),
            ((t >= last - h) & (h > 0), t - (last - h), from_right, 1, left, h == last),
        ):
            dest = jnp.clip(dest, 0, last)
            i = (k, c, lane, t)
            if t > 0:

                def forward(box=box, dest=dest, i=i, target=target):
                    box[k, c, t - 1] = box[k, c, t - 1] + parts[k, c, dest]
                    remote(
                        box.at[k, c, t - 1], box.at[k, c, t], rs_send.at[i], rs_recv.at[i], target
                    ).start()

                pl.when(on & jnp.logical_not(at_end))(forward)
            pl.when(on & at_end)(
                remote(
                    parts.at[k, c, dest], box.at[k, c, t], rs_send.at[i], rs_recv.at[i], target
                ).start
            )

    def rsw(k, c, t):
        for on, box, lane, target in (
            ((t >= h - 1) & (h > 0), from_left, 0, right),
            ((t >= last - h - 1) & (h < last), from_right, 1, left),
        ):
            i = (k, c, lane, t)
            block = box.at[k, c, t]
            pl.when(on)(remote(block, block, rs_send.at[i], rs_recv.at[i], target).wait_recv)

    def summed(k, c):
        zero = jnp.zeros((rc, model), f32)
        return (
            parts[k, c, h].astype(f32)
            + jnp.where(h > 0, from_left[k, c, last - 1].astype(f32), zero)
            + jnp.where(h < last, from_right[k, c, last - 1].astype(f32), zero)
        )

    def over_tiles(second, body, tile):
        whole_tiles, rest = units // tile, units % tile
        middle = (whole_tiles + 1) // 2

        def step(i, carry):
            body(pl.ds(pl.multiple_of(i * tile, tile), tile))
            return carry

        lax.fori_loop(middle if second else 0, whole_tiles if second else middle, step, 0)
        if second and rest:
            body(pl.ds(whole_tiles * tile, rest))

    arrived = set()

    def need(n):
        if n not in arrived:
            arrived.add(n)
            loads[n].wait()

    def span_rows(buf, p):
        return buf[pl.ds(p * each, each)].reshape(many, model)

    def place_parts(k, p, cols, value):
        parts[k, pl.ds(p * each, each), :, :, cols] = value.astype(bf16).reshape(
            each, heads, rc, value.shape[1]
        )

    def forward_tiles(c, second):
        need(0)
        need(1)

        def body(cols):
            u = span_rows(u_all, c)
            gate = contract_last(u, w_gate[cols, :])
            up = contract_last(u, w_up[cols, :])
            root = math.sqrt(2.0 / math.pi)
            square = gate * gate
            curve = jnp.tanh(root * gate * (1.0 + 0.044715 * square))
            half = 0.5 * (1.0 + curve)
            gelu = gate * half
            slope = half + 0.5 * gate * (1.0 - curve * curve) * (
                root * (1.0 + 3 * 0.044715 * square)
            )
            by_gate[pl.ds(c * many, many), cols] = slope * up
            by_up[pl.ds(c * many, many), cols] = gelu
            act[pl.ds(c * many, many), cols] = (gelu * up).astype(bf16)

        over_tiles(second, body, 512)

    wide = (model // 2 + 127) // 128 * 128

    def over_columns(body):
        body(pl.ds(0, wide))
        body(pl.ds(wide, model - wide))

    def down_rows(c):
        need(2)

        def body(cols):
            place_parts(
                0,
                c,
                cols,
                jnp.dot(
                    act[pl.ds(c * many, many), :], w_down[:, cols], preferred_element_type=f32
                ),
            )

        over_columns(body)

    def turn(c):
        here = pl.ds(c * rc, rc)
        ffn_out = summed(0, c)
        upstream = cot_ref[here, :].astype(f32)
        o_out[here, :] = (hidden[here, :] + norm_rows(ffn_out, flat(gain_four_ref))).astype(
            o_out.dtype
        )
        d_out, terms = back_norm(ffn_out, flat(gain_four_ref), upstream)
        d_all[c, h] = d_out.astype(bf16)
        o_gains[3:4, :] += terms

    def back_tiles(c, second):
        def body(cols):
            d_act = contract_last(span_rows(d_all, c), w_down[cols, :])
            d_gate[pl.ds(c * many, many), cols] = (
                d_act * by_gate[pl.ds(c * many, many), cols]
            ).astype(bf16)
            d_up[pl.ds(c * many, many), cols] = (
                d_act * by_up[pl.ds(c * many, many), cols]
            ).astype(bf16)

        over_tiles(second, body, 512)

    def back_rows(c):
        def body(cols):
            part = jnp.dot(
                d_gate[pl.ds(c * many, many), :], w_gate[:, cols], preferred_element_type=f32
            )
            part = part + jnp.dot(
                d_up[pl.ds(c * many, many), :], w_up[:, cols], preferred_element_type=f32
            )
            place_parts(1, c, cols, part)

        over_columns(body)

    def finish_rows(c):
        here = pl.ds(c * rc, rc)
        d_in, terms = back_norm(hidden[here, :], flat(gain_three_ref), summed(1, c))
        o_gains[2:3, :] += terms
        d_hid = cot_ref[here, :].astype(f32) + d_in
        o_hid[here, :] = d_hid
        d_proj, terms = back_norm(proj_ref[here, :], flat(gain_two_ref), d_hid)
        o_proj[here, :] = d_proj.astype(o_proj.dtype)
        o_gains[1:2, :] += terms

    stores = []

    def flip(source):
        for p in range(spans):
            flipped[:, pl.ds(p * many, many)] = span_rows(source, p).T

    def weight_grad(right_ref, dst, half):
        def body(cols):
            value = jnp.dot(flipped[...], right_ref[:, cols], preferred_element_type=f32)
            dst[:, :, cols] = value.astype(bf16).reshape(dst.shape[:2] + (value.shape[1],))

        over_tiles(half, body, 512)

    held = subsets(ups)
    sum_gate = Sum(links, lambda m: dw_gate.at[related(s, m)], box_gate, [0])
    sum_down = Sum(links, lambda m: dw_down.at[related(s, m)], box_down, [0])
    for total in (sum_gate, sum_down):
        total.masks = lambda stage: held
    def store(src, dst):
        copy = pltpu.make_async_copy(src, dst, local_sem.at[3 + len(stores)])
        copy.start()
        stores.append(copy)

    split = box_first.shape[1]
    pieces = []
    for box, order, low in ((box_first, ups, 0), (box_second, downs, split)):
        here = pl.ds(low, box.shape[1])
        pieces.append(
            Sum(links, lambda m, here=here: box_down.at[held.index(m), here], box, order)
        )

    for event in ORDER:
        kind, args = event[0], event[1:]
        if kind == "ags":
            ags(*args)
        elif kind == "agw":
            agw(*args)
        elif kind == "rss":
            rss(*args)
        elif kind == "rsw":
            rsw(*args)
        elif kind == "fa":
            forward_tiles(args[0], False)
        elif kind == "fb":
            forward_tiles(args[0], True)
        elif kind == "fc":
            down_rows(args[0])
        elif kind == "n":
            turn(args[0])
        elif kind == "ga":
            back_tiles(args[0], False)
        elif kind == "gb":
            back_tiles(args[0], True)
        elif kind == "gc":
            back_rows(args[0])
        elif kind == "e":
            finish_rows(args[0])
        elif kind == "wd":
            if args[0] == 0:
                flip(d_all)
            weight_grad(act, dw_down, args[0])
        elif kind == "wg":
            if args[0] == 0:
                flip(u_all)
            weight_grad(d_gate, dw_gate, args[0])
        elif kind == "wu":
            weight_grad(d_up, dw_up, args[0])
            if args[0] == 1:
                store(dw_up, o_up)
        elif kind == "dd":
            sum_down.start()
        elif kind == "dg":
            sum_gate.start()
        elif kind == "Dg":
            in_turn(sum_gate.steps(0))
            store(box_gate, o_gate)
        elif kind == "Dd":
            in_turn(sum_down.steps(0))
            for total in pieces:
                for m in total.masks(0):
                    total.send(0, m)
        else:
            for total, out in zip(pieces, (o_first, o_second)):
                for m in total.masks(0):
                    copy, where = total.waiting.pop((0, m))
                    copy.wait_recv()
                    total.boxes[where] = total.boxes[where] + total.current(m)[...]
                store(total.boxes, out)

    for event in ORDER:
        if event[0] == "ags":
            k, c, t = event[1:]
            for on, block, lane, target, _, _ in lanes(k, c, t):
                i = (k, c, lane, t)
                pl.when(on)(remote(block, block, ag_send.at[i], ag_recv.at[i], target).wait_send)
        elif event[0] == "rss":
            k, c, t = event[1:]
            for on, box, lane, target in (
                ((t >= h) & (h < last), from_left, 0, right),
                ((t >= last - h) & (h > 0), from_right, 1, left),
            ):
                i = (k, c, lane, t)
                block = box.at[k, c, t]
                pl.when(on)(remote(block, block, rs_send.at[i], rs_recv.at[i], target).wait_send)
    for n in range(3):
        need(n)
    for copy in stores:
        copy.wait()
    links.finish()


def feed_forward(nseq, heads, cid, *arrays):
    _, x, _, _, _, _, w_gate, w_up, w_down = arrays
    f32, bf16 = jnp.float32, jnp.bfloat16
    rows, model = x.shape
    units = w_gate.shape[0]
    chunks = CHUNKS
    rc = rows // chunks
    group = rows * heads
    vm = pl.BlockSpec(memory_space=VMEM)
    anywhere = pl.BlockSpec(memory_space=pl.ANY)
    block = (model // nseq, units)
    some = nseq // 2
    half = jax.ShapeDtypeStruct((some,) + block, bf16)
    split = split_rows(block[0])
    parts = [(split, units), (block[0] - split, units)]
    messages = 3 * some
    hops = (2, chunks, 2, heads - 1)
    return pl.pallas_call(
        functools.partial(ffn_kernel, nseq, heads, CHUNKS, SPANS),
        out_shape=[
            jax.ShapeDtypeStruct((rows, model), bf16),
            jax.ShapeDtypeStruct((rows, model), f32),
            jax.ShapeDtypeStruct((rows, model), bf16),
            jax.ShapeDtypeStruct((8, model), f32),
            *[jax.ShapeDtypeStruct((some // 2,) + part, bf16) for part in parts],
            half,
            jax.ShapeDtypeStruct((nseq,) + block, bf16),
        ],
        in_specs=[vm] * 6 + [anywhere] * 3,
        out_specs=[vm] * 4 + [anywhere] * 4,
        scratch_shapes=[
            VMEM((rows, model), f32),
            VMEM(w_gate.shape, bf16),
            VMEM(w_up.shape, bf16),
            VMEM(w_down.shape, bf16),
            VMEM((chunks, heads, rc, model), bf16),
            VMEM((chunks, heads, rc, model), bf16),
            VMEM((group, units), f32),
            VMEM((group, units), f32),
            VMEM((group, units), bf16),
            VMEM((group, units), bf16),
            VMEM((group, units), bf16),
            VMEM((2, chunks, heads, rc, model), bf16),
            VMEM((2, chunks, heads - 1, rc, model), bf16),
            VMEM((2, chunks, heads - 1, rc, model), bf16),
            VMEM((model, group), bf16),
            VMEM((nseq,) + block, bf16),
            VMEM((nseq,) + block, bf16),
            VMEM((nseq,) + block, bf16),
            VMEM((some,) + block, bf16),
            VMEM((some,) + block, bf16),
            *[VMEM((some // 2,) + part, bf16) for part in parts],
            pltpu.SemaphoreType.DMA((messages,)),
            pltpu.SemaphoreType.DMA((messages,)),
            pltpu.SemaphoreType.DMA(hops),
            pltpu.SemaphoreType.DMA(hops),
            pltpu.SemaphoreType.DMA(hops),
            pltpu.SemaphoreType.DMA(hops),
            pltpu.SemaphoreType.DMA((7,)),
        ],
        name="feed_forward",
        compiler_params=pltpu.CompilerParams(
            collective_id=cid, has_side_effects=True, vmem_limit_bytes=62 * 2**20
        ),
    )(*arrays)


def finish_kernel(nseq, qw, width, each, few, *refs):
    out, tokens, qkv, w_out, gate, up, down, gains = refs[:8]
    o_out, o_tokens, o_query, o_key, o_value, o_w_out, o_gate, o_up, o_down = refs[8:17]
    o_gains = refs[17:]
    s, h = place()
    which = s * lax.axis_size("head") + h
    o_out[...] = out[...]
    o_tokens[...] = tokens[...]
    o_query[...] = qkv[:, :qw]
    o_key[...] = qkv[:, qw : qw + width]
    o_value[...] = qkv[:, qw + width :]
    o_w_out[...] = w_out[...]
    o_gate[...] = gate[...].astype(jnp.float32)
    o_up[...] = up[...].astype(jnp.float32)
    o_down[...] = down[...].astype(jnp.float32)
    model = gains.shape[1]
    wide = pltpu.roll(gains[...], lax.rem(model - which * each, model), 1)
    narrow = pltpu.roll(gains[...], lax.rem(model - which * few, model), 1)
    for i in range(4):
        o_gains[i][...] = wide[i : i + 1, :each]
    for i in range(4, 6):
        o_gains[i][...] = narrow[i : i + 1, :few]


def finish(nseq, qw, width, each, few, *arrays):
    out, tokens, qkv, w_out, gate, up, down, gains = arrays
    vm = pl.BlockSpec(memory_space=VMEM)
    shape = lambda a: jax.ShapeDtypeStruct(a.shape, a.dtype)
    f32 = jnp.float32
    rows = qkv.shape[0]
    wide, narrow = jax.ShapeDtypeStruct((1, each), f32), jax.ShapeDtypeStruct((1, few), f32)
    return pl.pallas_call(
        functools.partial(finish_kernel, nseq, qw, width, each, few),
        out_shape=[shape(out), shape(tokens)]
        + [jax.ShapeDtypeStruct((rows, n), f32) for n in (qw, width, width)]
        + [jax.ShapeDtypeStruct(a.shape, f32) for a in (w_out, gate, up, down)]
        + [wide] * 4
        + [narrow] * 2,
        in_specs=[vm] * 8,
        out_specs=[vm] * 15,
        name="finish",
        compiler_params=pltpu.CompilerParams(vmem_limit_bytes=LIMIT),
    )(*arrays)


def local(
    tokens,
    segment_ids,
    w_query,
    w_key,
    w_value,
    w_out,
    w_gate,
    w_up,
    w_down,
    gain_attn_in,
    gain_attn_out,
    gain_ffn_in,
    gain_ffn_out,
    gain_query,
    gain_key,
    cotangent,
):
    heads = lax.axis_size("head")
    nseq = lax.axis_size("seq")
    head_index = lax.axis_index("head")
    seq_index = lax.axis_index("seq")
    bits = nseq.bit_length() - 1
    local_rows, model = tokens.shape
    width = gain_query.shape[0]
    qcount = w_query.shape[1] // width
    group = local_rows * heads
    total = segment_ids.shape[0]
    hidden_units = w_gate.shape[1]
    scale = 1.0 / math.sqrt(width)
    bf16 = jnp.bfloat16
    if (nseq, heads) == (8, 4) and (model // nseq) % 16 == 0:
        qw = qcount * width
        each, few = model // (nseq * heads), width // (nseq * heads)
        (
            projected,
            queries,
            keys,
            values,
            starts,
            index,
            log_total,
            attended_t,
            q_linear,
            k_linear,
            cosines,
            sines,
            attn_t,
        ) = front(
            nseq,
            heads,
            qcount,
            scale,
            11,
            tokens,
            segment_ids,
            w_key,
            w_value,
            gain_attn_in,
            gain_query,
            gain_key,
            w_query,
            w_out,
        )
        output, d_hidden, d_projected, gains, down_first, down_second, half_gate, all_up = feed_forward(
            nseq,
            heads,
            10,
            projected,
            tokens,
            cotangent,
            gain_attn_out,
            gain_ffn_in,
            gain_ffn_out,
            w_gate.T,
            w_up.T,
            w_down,
        )
        grad_tokens, sum_qkv, sum_out, sum_gate, sum_up, sum_down, sum_gains = tail(
            nseq,
            heads,
            qcount,
            scale,
            9,
            queries,
            starts,
            index,
            log_total,
            attended_t,
            d_projected,
            k_linear,
            cosines,
            sines,
            gain_query,
            gain_key,
            gain_attn_in,
            gains,
            keys.reshape(nseq, group, width),
            values.reshape(nseq, group, width),
            w_out,
            q_linear,
            attn_t,
            tokens,
            d_hidden,
            w_query,
            w_key,
            w_value,
            half_gate,
            all_up,
            down_first,
            down_second,
        )
        (
            output,
            grad_tokens,
            sum_query,
            sum_key,
            sum_value,
            sum_out,
            sum_gate,
            sum_up,
            sum_down,
            *sum_gains,
        ) = finish(
            nseq,
            qw,
            width,
            each,
            few,
            output,
            grad_tokens,
            sum_qkv,
            sum_out,
            sum_gate,
            sum_up,
            sum_down,
            sum_gains,
        )
        return (
            output,
            grad_tokens,
            sum_query,
            sum_key,
            sum_value,
            sum_out,
            sum_gate,
            sum_up,
            sum_down.T,
            *[g[0] for g in sum_gains],
        )
    first_row = (seq_index * heads + head_index) * local_rows
    my_index = first_row + jnp.arange(local_rows, dtype=jnp.int32)
    my_ids = lax.dynamic_slice_in_dim(segment_ids, first_row, local_rows)
    my_starts = jnp.min(
        jnp.where(
            my_ids[:, None] == segment_ids[None, :],
            jnp.arange(total, dtype=jnp.int32)[None, :],
            total,
        ),
        axis=1,
    )
    cosines, sines = rope_tables(my_index - my_starts, width)

    def query_path(linear, gain):
        shaped = linear.reshape(local_rows, qcount, width)
        turned = rotate(norm_rows(shaped, gain), cosines[:, None, :], sines[:, None, :])
        return turned.reshape(local_rows, qcount * width)

    def key_path(linear, gain):
        return rotate(norm_rows(linear, gain), cosines, sines)

    def gated(gate, up):
        return jax.nn.gelu(gate, approximate=True) * up

    def stacked(v):
        return v.reshape(local_rows, qcount, width).transpose(1, 0, 2).reshape(-1, width)

    def unstacked(v):
        return v.reshape(qcount, local_rows, width).transpose(1, 0, 2).reshape(local_rows, -1)

    inputs = tokens.astype(jnp.float32)
    attn_in = norm_rows(inputs, gain_attn_in).astype(bf16)
    k_linear = jnp.dot(attn_in, w_key, preferred_element_type=jnp.float32)
    keys_local = key_path(k_linear, gain_key).astype(bf16)
    values_local = jnp.dot(attn_in, w_value, preferred_element_type=jnp.float32).astype(bf16)
    q_linear = jnp.dot(attn_in, w_query, preferred_element_type=jnp.float32)
    queries_local = query_path(q_linear, gain_query).astype(bf16)
    queries = stacked(queries_local) * jnp.asarray(scale, bf16)
    keys, values = gather_all([keys_local, values_local], nseq, heads, 1)
    keys = keys.reshape(nseq, group, width)
    values = values.reshape(nseq, group, width)
    starts = jnp.tile(my_starts, qcount)[None, :]
    index = jnp.tile(my_index, qcount)[None, :]
    attended_t, log_total = attend(queries, keys, values, starts, index)
    attended = attended_t.T
    mixed_local = unstacked(attended.astype(bf16))
    projected = jnp.dot(mixed_local, w_out, preferred_element_type=jnp.float32)
    hidden = inputs + norm_rows(projected, gain_attn_out)
    ffn_in = norm_rows(hidden, gain_ffn_in).astype(bf16)
    ffn_rows = line_gather(ffn_in, heads, 2).reshape(group, model)
    gate = jnp.dot(ffn_rows, w_gate, preferred_element_type=jnp.float32)
    up = jnp.dot(ffn_rows, w_up, preferred_element_type=jnp.float32)
    activated = gated(gate, up).astype(bf16)
    ffn_out = line_scatter(
        jnp.dot(activated, w_down, preferred_element_type=jnp.float32)
        .astype(bf16)
        .reshape(heads, local_rows, model),
        heads,
        3,
    )
    output = hidden + norm_rows(ffn_out, gain_ffn_out)
    upstream = cotangent.astype(jnp.float32)
    unused, back_four = jax.vjp(norm_rows, ffn_out, gain_ffn_out)
    d_ffn_out, d_gain_four = back_four(upstream)
    d_ffn_rows = line_gather(d_ffn_out.astype(bf16), heads, 4).reshape(group, model)
    d_activated = contract_last(d_ffn_rows, w_down)
    d_w_down = contract_first(d_ffn_rows, activated)
    unused, back_gate = jax.vjp(gated, gate, up)
    d_gate, d_up = back_gate(d_activated)
    d_gate = d_gate.astype(bf16)
    d_up = d_up.astype(bf16)
    d_ffn_in = line_scatter(
        (contract_last(d_gate, w_gate) + contract_last(d_up, w_up))
        .astype(bf16)
        .reshape(heads, local_rows, model),
        heads,
        5,
    )
    d_w_gate = contract_first(ffn_rows, d_gate)
    d_w_up = contract_first(ffn_rows, d_up)
    unused, back_three = jax.vjp(norm_rows, hidden, gain_ffn_in)
    d_hidden_part, d_gain_three = back_three(d_ffn_in)
    d_hidden = upstream + d_hidden_part
    unused, back_two = jax.vjp(norm_rows, projected, gain_attn_out)
    d_projected, d_gain_two = back_two(d_hidden)
    d_projected = d_projected.astype(bf16)
    qw = qcount * width
    d_w_out = contract_first(mixed_local, d_projected)
    d_mixed = contract_last(d_projected, w_out).astype(bf16)
    grad_attended = stacked(d_mixed)
    row_dots = jnp.sum(grad_attended.astype(jnp.float32) * attended, axis=1)[None, :]
    d_queries_t, d_keys, d_values = attend_back(
        queries, keys, values, starts, index, log_total, row_dots, grad_attended
    )
    shape = (nseq, heads, local_rows, width)
    ups, downs = seq_orders(bits)
    d_keys, d_values = scatter_all(
        [d_keys.reshape(shape), d_values.reshape(shape)],
        [True, True],
        [[0] + ups, [0] + downs],
        nseq,
        heads,
        6,
        "scatter_keys",
    )
    d_query_rot = unstacked((d_queries_t.T * scale).astype(bf16)).astype(jnp.float32)
    unused, back_query = jax.vjp(query_path, q_linear, gain_query)
    d_q_linear, d_gain_query = back_query(d_query_rot)
    unused, back_key = jax.vjp(key_path, k_linear, gain_key)
    d_k_linear, d_gain_key = back_key(d_keys)
    d_qkv = jnp.concatenate([d_q_linear, d_k_linear, d_values], axis=1).astype(bf16)
    qw = qcount * width
    d_w_qkv = contract_first(attn_in, d_qkv)
    d_attn_in = (
        contract_last(d_qkv[:, :qw], w_query)
        + contract_last(d_qkv[:, qw : qw + width], w_key)
        + contract_last(d_qkv[:, qw + width :], w_value)
    )
    unused, back_one = jax.vjp(norm_rows, inputs, gain_attn_in)
    d_inputs, d_gain_one = back_one(d_attn_in)
    grad_tokens = (d_hidden + d_inputs).astype(bf16)

    def cut(v):
        return v.reshape(nseq, heads, -1)

    wide = jnp.stack([cut(d_gain_one), cut(d_gain_two), cut(d_gain_three), cut(d_gain_four)], 2)
    narrow = jnp.stack([cut(d_gain_query), cut(d_gain_key)], 2)
    each, few = wide.shape[-1], narrow.shape[-1]
    gains = jnp.concatenate(
        [
            jnp.pad(wide, ((0, 0), (0, 0), (0, 0), (0, 128 - each))),
            jnp.pad(narrow, ((0, 0), (0, 0), (0, 2), (0, 128 - few))),
        ],
        axis=2,
    )
    sum_qkv, sum_out, sum_gains = scatter_all(
        [
            d_w_qkv.astype(bf16).reshape(nseq, heads, -1, d_qkv.shape[1]),
            d_w_out.astype(bf16).reshape(nseq, heads, -1, model),
            gains,
        ],
        [True, True, True],
        [[0] + ups, [0] + downs, [0] + downs],
        nseq,
        heads,
        7,
        "scatter_attn",
    )
    sum_gate, sum_up, sum_down = scatter_all(
        [
            d.astype(bf16).reshape(nseq, model // nseq, hidden_units)
            for d in (d_w_gate, d_w_up, d_w_down)
        ],
        [False, False, False],
        [[0] + ups, [0] + downs, [0] + ups],
        nseq,
        heads,
        8,
        "scatter_ffn",
    )
    return (
        output.astype(bf16),
        grad_tokens,
        sum_qkv[:, :qw],
        sum_qkv[:, qw : qw + width],
        sum_qkv[:, qw + width :],
        sum_out,
        sum_gate,
        sum_up,
        sum_down.T,
        sum_gains[0, :each],
        sum_gains[1, :each],
        sum_gains[2, :each],
        sum_gains[3, :each],
        sum_gains[4, :few],
        sum_gains[5, :few],
    )


def solution(mesh):
    rows = P(("seq", "head"), None)
    in_specs = (
        rows,
        P(),
        P(),
        P(),
        P(),
        P(),
        P(None, "head"),
        P(None, "head"),
        P("head", None),
        P(),
        P(),
        P(),
        P(),
        P(),
        P(),
        rows,
    )
    out_specs = (
        rows,
        rows,
        rows,
        rows,
        rows,
        rows,
        P("seq", "head"),
        P("seq", "head"),
        P("head", "seq"),
    ) + (P(("seq", "head")),) * 6
    return jax.shard_map(local, mesh=mesh, in_specs=in_specs, out_specs=out_specs, check_vma=False)
```

profile of v0, /device:TPU:0, one launch (start us, length us, event | category | flops | bytes accessed | tf_op | source)
XLA Modules:
  0.0 215.1 jit_solution(47896783522276630)
XLA Ops:
  0.6 34.0 %front.1 = (f32[128,1152]{1,0:T(8,128)}, bf16[512,256]{1,0:T(8,128)(2,1)}, bf16[8,4,128,256]{3,2,1,0:T(8,128)(2,1)}, bf16[8,4,128,256]{3,2,1,0:T(8,128)(2,1)}, s...) custom-call(bf16[128,1152]{1,0:T(8,128)(2,1)} %refs_18_.1, ...), custom_call_target="tpu_custom_call" | custom-call | tf_op jit(solution)/shard_map/front/pallas_call | solution.py:733
  34.7 88.8 %feed_forward.1 = (bf16[128,1152]{1,0:T(8,128)(2,1)}, f32[128,1152]{1,0:T(8,128)}, bf16[128,1152]{1,0:T(8,128)(2,1)}, f32[8,1152]{1,0:T(8,128)}, bf16[2,80,1728]...) custom-call(f32[128,1152]{1,0:T(8,128)} %get-tuple-element.58.proj_r, ...), custom_call_target="tpu_custom_call" | custom-call | tf_op jit(solution)/shard_map/feed_forward/pallas_call | solution.py:1786
  123.4 87.7 %tail.1 = (bf16[128,1152]{1,0:T(8,128)(2,1)}, f32[36,1536]{1,0:T(8,128)}, f32[32,1152]{1,0:T(8,128)}, bf16[144,1728]{1,0:T(8,128)(2,1)}, bf16[144,1728]{1,0:T(8,...) custom-call(bf16[512,256]{1,0:T(8,128)(2,1)} %get-tuple-element.60.refs_0_, s32[1,512]{1,0:T(1,128)} %get-tuple-element.61.refs_1_, ...), custom_call_target="tpu_custom_call" | custom-call | tf_op jit(solution)/shard_map/tail/pallas_call | solution.py:1307
  211.2 3.7 %finish.1 = (bf16[128,1152]{1,0:T(8,128)(2,1)}, bf16[128,1152]{1,0:T(8,128)(2,1)}, f32[36,1024]{1,0:T(8,128)}, f32[36,256]{1,0:T(8,128)}, f32[36,256]{1,0:T(8,12...) custom-call(bf16[128,1152]{1,0:T(8,128)(2,1)} %get-tuple-element.59., ...), custom_call_target="tpu_custom_call" | custom-call | tf_op jit(solution)/shard_map/finish/pallas_call | solution.py:1867
where the time goes:
time: 215 us
  Pallas kernels  214 us (100%)
    pallas_call x1, Pallas kernels, feed_forward(): pl.pallas_call(functools.partial(ffn_kernel, nseq, heads, CHUNKS, SPANS),...  88.8 us
    pallas_call x1, Pallas kernels, tail(): pl.pallas_call(kernel, out_shape=[jax.ShapeDtypeStruct((rows, model), bf1...  87.7 us
    pallas_call x1, Pallas kernels, front(): pl.pallas_call(kernel, out_shape=[shape((rows, model), f32), shape((stack...  34 us

commit v1 on v0

--- a/solution.py
+++ b/solution.py
@@ -692,13 +692,13 @@
     )
     for copy in pairs:
         copy.wait_recv()
-    mass = lax.fori_loop(
-        0, s // 2 + low, lambda i, m: attend_group(2 * i + 1 - low, m), mass
-    )
     keep_k = pltpu.make_async_copy(k_all, o_k, local_sem.at[2])
     keep_v = pltpu.make_async_copy(v_all, o_v, local_sem.at[3])
     keep_k.start()
     keep_v.start()
+    mass = lax.fori_loop(
+        0, s // 2 + low, lambda i, m: attend_group(2 * i + 1 - low, m), mass
+    )
     o_log[...] = jnp.log(mass)
     attended = o_att[...] / mass
     o_att[...] = attended

time: 215 us -> 214 us (level)
  no operation moved by 1% of the time
where the time goes in v1:
time: 214 us; the launch traced here: 213 us
  Pallas kernels  213 us (100%)
    pallas_call x1, Pallas kernels, feed_forward(): pl.pallas_call(functools.partial(ffn_kernel, nseq, heads, CHUNKS, SPANS),...  87.7 us
    pallas_call x1, Pallas kernels, tail(): pl.pallas_call(kernel, out_shape=[jax.ShapeDtypeStruct((rows, model), bf1...  87.2 us
    pallas_call x1, Pallas kernels, front(): pl.pallas_call(kernel, out_shape=[shape((rows, model), f32), shape((stack...  34 us

profile of v1, /device:TPU:0, one launch (start us, length us, event | category | flops | bytes accessed | tf_op | source)
XLA Modules:
  0.0 213.4 jit_solution(16672094030114224588)
XLA Ops:
  0.6 34.0 %front.1 = (f32[128,1152]{1,0:T(8,128)}, bf16[512,256]{1,0:T(8,128)(2,1)}, bf16[8,4,128,256]{3,2,1,0:T(8,128)(2,1)}, bf16[8,4,128,256]{3,2,1,0:T(8,128)(2,1)}, s...) custom-call(bf16[128,1152]{1,0:T(8,128)(2,1)} %refs_18_.1, ...), custom_call_target="tpu_custom_call" | custom-call | tf_op jit(solution)/shard_map/front/pallas_call | solution.py:733
  34.7 87.7 %feed_forward.1 = (bf16[128,1152]{1,0:T(8,128)(2,1)}, f32[128,1152]{1,0:T(8,128)}, bf16[128,1152]{1,0:T(8,128)(2,1)}, f32[8,1152]{1,0:T(8,128)}, bf16[2,80,1728]...) custom-call(f32[128,1152]{1,0:T(8,128)} %get-tuple-element.58.proj_r, ...), custom_call_target="tpu_custom_call" | custom-call | tf_op jit(solution)/shard_map/feed_forward/pallas_call | solution.py:1786
  122.3 87.2 %tail.1 = (bf16[128,1152]{1,0:T(8,128)(2,1)}, f32[36,1536]{1,0:T(8,128)}, f32[32,1152]{1,0:T(8,128)}, bf16[144,1728]{1,0:T(8,128)(2,1)}, bf16[144,1728]{1,0:T(8,...) custom-call(bf16[512,256]{1,0:T(8,128)(2,1)} %get-tuple-element.60.refs_0_, s32[1,512]{1,0:T(1,128)} %get-tuple-element.61.refs_1_, ...), custom_call_target="tpu_custom_call" | custom-call | tf_op jit(solution)/shard_map/tail/pallas_call | solution.py:1307
  209.5 3.7 %finish.1 = (bf16[128,1152]{1,0:T(8,128)(2,1)}, bf16[128,1152]{1,0:T(8,128)(2,1)}, f32[36,1024]{1,0:T(8,128)}, f32[36,256]{1,0:T(8,128)}, f32[36,256]{1,0:T(8,12...) custom-call(bf16[128,1152]{1,0:T(8,128)(2,1)} %get-tuple-element.59., ...), custom_call_target="tpu_custom_call" | custom-call | tf_op jit(solution)/shard_map/finish/pallas_call | solution.py:1867
